TPU v7x, 512 devices: a whole 4x4x16 slice. The times are simulated.
512 devices in a mesh: seq: 64 (over y, x, z_lo), head: 8 (over z_hi, core).
Axes of the slice: x: 4, y: 4, z: 16 (z_hi: 4, z_lo: 4; z = z_hi * 4 + z_lo), core: 2. Of those that a mesh axis runs over, the one named last changes fastest.
Arguments:
- queries: bfloat16 [16384, 5120], P('seq', 'head'), may hold values from -100 to 100
- keys: bfloat16 [16384, 5120], P('seq', 'head'), may hold values from -12 to 12
- values: bfloat16 [16384, 5120], P('seq', 'head'), may hold values from -6 to 6
- hidden: bfloat16 [16384, 5120], P('seq', 'head'), may hold values from -3 to 3
- cached: bfloat16 [16384, 5120], P('seq', 'head'), may hold values from -6 to 6
- active: int32 [16384], P('seq'), may hold values from 0 to 1, as said below
- w_out: bfloat16 [5120, 5120], P('head', 'seq'), may hold values from -0.078125 to 0.078125
Outputs:
- block_output: bfloat16 [16384, 5120], P('seq', 'head')
Inputs may be any that keep to these rules, and one draw needn't show every extreme that they name: `active`: exactly 704 ones in all; among the 256 tokens of one index of seq at most 32 ones, and that many on some of them.
All inputs are finite; a program needn't handle non-finite values.
Results may differ from a plain program's by a relative error of at most 0.0039.
Values may be sent and summed in bfloat16 or wider, within the bound.
A program may use at most 64 MiB of HBM per device.

v0:
```python
import jax
import jax.numpy as jnp
from jax import lax
from jax.sharding import PartitionSpec as P

HD = 128


def for_sending(value):

    def short(part):
        return part.astype(jnp.bfloat16) if part.dtype == jnp.float32 else part

    return jax.tree.map(short, value)


def local_partials(query_rows, keys, values):
    head_count = keys.shape[1] // HD
    inv_root = 1.0 / HD**0.5

    def one_head(head):
        start = head * HD
        q_head = lax.dynamic_slice_in_dim(query_rows, start, HD, 1)
        k_head = lax.dynamic_slice_in_dim(keys, start, HD, 1)
        v_head = lax.dynamic_slice_in_dim(values, start, HD, 1)
        scores = (
            lax.dot_general(
                q_head, k_head, (((1,), (1,)), ((), ())), preferred_element_type=jnp.float32
            )
            * inv_root
        )
        peak = jnp.max(scores, axis=1)
        expo = jnp.exp(scores - peak[:, None])
        total = jnp.sum(expo, axis=1)
        block_out = jnp.dot(expo.astype(jnp.bfloat16), v_head, preferred_element_type=jnp.float32)
        return ((block_out / total[:, None]).astype(jnp.bfloat16), peak, total)

    return lax.map(one_head, jnp.arange(head_count, dtype=jnp.int32))


def shards(queries, keys, values, hidden, cached, active, w_out):
    tok_dev, features = queries.shape
    head_count = features // HD
    devices = lax.axis_size("seq")
    capacity = tok_dev // 8
    act_rows = jnp.nonzero(active, size=capacity, fill_value=tok_dev)[0].astype(jnp.int32)
    safe_rows = jnp.minimum(act_rows, tok_dev - 1)
    own_queries = queries[safe_rows]
    gathered = lax.all_gather(own_queries, "seq", axis=0, tiled=True)
    block_out, block_peak, block_total = local_partials(gathered, keys, values)
    block_out = block_out.reshape(head_count, devices, capacity, HD)
    peak_in, total_in = (
        lax.all_to_all(
            block_peak.reshape(head_count, devices, capacity),
            "seq",
            split_axis=1,
            concat_axis=1,
            tiled=True,
        ),
        lax.all_to_all(
            block_total.reshape(head_count, devices, capacity),
            "seq",
            split_axis=1,
            concat_axis=1,
            tiled=True,
        ),
    )
    out_in = lax.all_to_all(
        for_sending(block_out), "seq", split_axis=1, concat_axis=1, tiled=True
    ).astype(block_out.dtype)
    top_max = jnp.max(peak_in, axis=1, keepdims=True)
    weight = total_in * jnp.exp(peak_in - top_max)
    mixed = jnp.einsum("hnc,hncd->hcd", weight, out_in.astype(jnp.float32))
    mixed = mixed / jnp.sum(weight, axis=1)[:, :, None]
    attn = jnp.transpose(mixed, (1, 0, 2)).reshape(capacity, features).astype(jnp.bfloat16)
    terms = jnp.dot(
        attn, lax.all_gather(w_out, "seq", axis=1, tiled=True), preferred_element_type=jnp.float32
    )
    summed = lax.psum_scatter(
        terms.astype(jnp.bfloat16), "head", scatter_dimension=1, tiled=True
    ).astype(jnp.float32)
    updated = (hidden[safe_rows].astype(jnp.float32) + summed).astype(jnp.bfloat16)
    return cached.at[act_rows].set(updated, mode="drop")


def solution(mesh):
    placed = (
        P("seq", "head"),
        P("seq", "head"),
        P("seq", "head"),
        P("seq", "head"),
        P("seq", "head"),
        P("seq"),
        P("head", "seq"),
    )
    return jax.shard_map(
        shards, mesh=mesh, in_specs=placed, out_specs=P("seq", "head"), check_vma=False
    )
```

profile of v0, /device:TPU:1, one launch (start us, length us, event | category | flops | bytes accessed | tf_op | source)
XLA Modules:
  0.0 835.7 jit_solution(14401901333159567819)
XLA Ops:
  6.5 1.8 copy.56
  8.3 0.7 fusion.24
  9.0 1.4 fusion.25
  10.4 0.3 reduce-window.12
  11.0 2.3 scatter_custom_fusion
  13.5 1.3 fusion.23
  14.8 2.3 gather_fusion
  17.2 0.7 all-gather.4.cloned.1.call-update
  17.9 318.7 %all-gather.6.cloned.1.call-done = bf16[2048,640]{1,0:T(8,128)(2,1)} async-done(((bf16[32,640]{1,0:T(8,128)(2,1)}), bf16[2048,640]{1,0:T(8,128)(2,1)}) %all-gather.6.cloned.1.call-update) | async-done | bytes 2621456 | tf_op jit(solution)/shard_map/all_gather | solution.py:49
  336.5 25.5 %while.14 = (s32[]{:T(128)}, bf16[5,2048,128]{2,1,0:T(8,128)(2,1)S(1)}, f32[5,2048]{1,0:T(8,128)S(1)}, f32[5,2048]{1,0:T(8,128)S(1)}, s32[5]{0:T(128)S(1)}, /*in...) while((s32[]{:T(128)}, ...), condition=%wide.region_8.9_spmd, body=%wide.region_5.8_spmd.sunk | while | flops 272101376 | bytes 7546555 | solution.py:38
  336.5 0.6 dynamic_slice.30
  337.8 1.5 fusion.39
  339.3 0.3 fusion.40
  339.6 1.6 fusion.41
  341.2 0.2 dynamic_update_slice.17
  341.4 0.2 dynamic_update_slice.16
  341.6 0.6 dynamic_slice.30
  342.9 1.5 fusion.39
  344.4 0.3 fusion.40
  344.7 1.6 fusion.41
  346.3 0.2 dynamic_update_slice.17
  346.5 0.2 dynamic_update_slice.16
  346.7 0.6 dynamic_slice.30
  348.0 1.5 fusion.39
  349.5 0.3 fusion.40
  349.8 1.6 fusion.41
  351.4 0.2 dynamic_update_slice.17
  351.6 0.2 dynamic_update_slice.16
  351.9 0.6 dynamic_slice.30
  353.1 1.5 fusion.39
  354.6 0.3 fusion.40
  354.9 1.6 fusion.41
  356.5 0.2 dynamic_update_slice.17
  356.7 0.2 dynamic_update_slice.16
  357.0 0.6 dynamic_slice.30
  358.2 1.5 fusion.39
  359.7 0.3 fusion.40
  360.0 1.6 fusion.41
  361.6 0.2 dynamic_update_slice.17
  361.8 0.2 dynamic_update_slice.16
  362.3 0.8 reshape.196
  363.0 7.7 all-to-all-start.2
  370.9 0.8 reshape.194
  371.7 7.9 all-to-all-done.2
  379.6 4.6 all-to-all-start.1
  384.2 2.0 copy.16
  386.2 6.8 all-to-all-done.1
  393.0 4.7 all-to-all-start
  397.8 0.5 broadcast.202
  398.3 0.8 reduce.6
  399.2 0.8 reduce.7
  400.1 0.7 bitcast_reduce_fusion
  400.7 1.4 fusion.16
  402.1 1.1 copy.22
  403.2 1.4 fusion.15
  404.5 0.8 copy.20
  405.3 55.5 %all-to-all-done = bf16[5,64,32,128]{3,2,0,1:T(8,128)(2,1)S(1)} async-done(((bf16[5,64,32,128]{3,2,0,1:T(8,128)(2,1)}), bf16[5,64,32,128]{3,2,0,1:T(8,128)(2,1)S(1)}, u32[]{:S(2)}, u32[]{:S(2)}) %all-to-all-start) | async-done | bytes 2621472 | tf_op jit(solution)/shard_map/all_to_all | solution.py:68
  460.8 1.4 fusion.12
  462.3 259.2 %all-gather.4.cloned.1.call-done = bf16[640,5120]{0,1:T(8,128)(2,1)} async-done(((bf16[640,80]{0,1:T(8,128)(2,1)}), bf16[640,5120]{0,1:T(8,128)(2,1)}) %all-gather.4.cloned.1.call-update) | async-done | bytes 6553616 | tf_op jit(solution)/shard_map/all_gather | solution.py:77
  721.5 4.9 convolution_convert_fusion
  726.5 1.4 copy.24
  727.9 97.5 %reduce-scatter.4.cloned.1.call-done = bf16[640,32]{1,0:T(8,128)(2,1)} async-done(((bf16[5120,32]{1,0:T(8,128)(2,1)}), bf16[640,32]{1,0:T(8,128)(2,1)}) %reduce-scatter.4.cloned.1.call-update) | async-done | bytes 40976
  825.4 1.0 copy.25
  826.5 2.7 scatter_custom_fusion.1
  (31 shorter events, 1.3 us)
Async XLA Ops:
  6.5 819.9 %copy-start = (bf16[256,640]{1,0:T(8,128)(2,1)S(1)}, bf16[256,640]{1,0:T(8,128)(2,1)}, u32[]{:S(2)}) copy-start(bf16[256,640]{1,0:T(8,128)(2,1)} %param.12) | copy-start | bytes 983044
  6.5 330.0 %all-gather.6.cloned.1.call-start = ((), (), s32[]{:S(2)}) async-start(), calls=%async_computation.5 | async-start | bytes 2662400 | tf_op jit(solution)/shard_map/all_gather | solution.py:49
  14.8 2.3 copy-start.1
  17.1 704.4 %all-gather.4.cloned.1.call-start = ((), (), s32[]{:S(2)}) async-start(), calls=%async_computation.4 | async-start | bytes 6656000 | tf_op jit(solution)/shard_map/all_gather | solution.py:77
  363.0 16.5 %all-to-all-start.2 = ((f32[64,1,160]{2,1,0:T(1,128)}), f32[64,1,160]{2,1,0:T(1,128)S(1)}, u32[]{:S(2)}, u32[]{:S(2)}) async-start(f32[64,1,160]{2,1,0:T(1,128)} %reshape.196), calls=%async_computation.2 | async-start | bytes 131072 | tf_op jit(solution)/shard_map/all_to_all | solution.py:53
  379.6 13.5 %all-to-all-start.1 = ((f32[64,1,160]{2,1,0:T(1,128)}), f32[64,1,160]{2,1,0:T(1,128)S(1)}, u32[]{:S(2)}, u32[]{:S(2)}) async-start(f32[64,1,160]{2,1,0:T(1,128)} %reshape.194), calls=%async_computation.1 | async-start | bytes 131072 | tf_op jit(solution)/shard_map/all_to_all | solution.py:60
  393.0 67.8 %all-to-all-start = ((bf16[5,64,32,128]{3,2,0,1:T(8,128)(2,1)}), bf16[5,64,32,128]{3,2,0,1:T(8,128)(2,1)S(1)}, u32[]{:S(2)}, u32[]{:S(2)}) async-start(bf16[5,64,32,128]{3,2,0,1:T(8,128)(2,1)} %copy.16), calls=%async_computation | async-start | bytes 5242880 | tf_op jit(solution)/shard_map/all_to_all | solution.py:68
  397.7 427.7 %reduce-scatter.4.cloned.1.call-start = ((), (), s32[]{:S(2)}) async-start(), calls=%async_computation.6 | async-start | bytes 1474560
  726.4 100.0 %copy-start.2 = (s32[1024]{0:T(1024)S(1)}, s32[1024]{0:T(1024)}, u32[]{:S(2)}) copy-start(s32[1024]{0:T(1024)} %copy-done.1) | copy-start | bytes 12292
Sparse Core Ops, SparseCore 0:
  17.2 319.2 all-gather.5
  338.6 382.8 all-gather.3
  728.0 97.3 reduce-scatter.3
where the time goes:
time: 837 us; the launch traced here: 836 us
  waiting for transfers between devices  746 us (89%)
  matrix products  21.9 us (3%)
  local copies, waits for them, and re-layouts  18.3 us (2%)
  starting transfers between devices  17.1 us (2%)
  other arithmetic  15.5 us (2%)
  between operations  13.3 us (2%)
    all_gather x1, waiting for transfers between devices, shards(): gathered = lax.all_gather(own_queries, 'seq', axis=0, tiled=True)  319 us
    all_gather x1, waiting for transfers between devices, shards(): lax.all_gather(w_out, 'seq', axis=1, tiled=True)  259 us
    unnamed x4, waiting for transfers between devices  98.2 us
    all_to_all x1, waiting for transfers between devices, shards(): lax.all_to_all(for_sending(block_out), 'seq', split_axis=1, concat_axis=1...  55.5 us
  transfers between devices with their start and end apart: 6, of which 6 were waited for; matrix products, arithmetic and copies ran while one was open for 4% of the time, Pallas kernels for 0%

commit v1 on v0

--- a/solution.py
+++ b/solution.py
@@ -74,7 +74,11 @@
     mixed = mixed / jnp.sum(weight, axis=1)[:, :, None]
     attn = jnp.transpose(mixed, (1, 0, 2)).reshape(capacity, features).astype(jnp.bfloat16)
     terms = jnp.dot(
-        attn, lax.all_gather(w_out, "seq", axis=1, tiled=True), preferred_element_type=jnp.float32
+        attn,
+        jnp.concatenate(
+            lax.all_to_all(jnp.stack([w_out] * lax.axis_size("seq")), "seq", 0, 0), axis=1
+        ),
+        preferred_element_type=jnp.float32,
     )
     summed = lax.psum_scatter(
         terms.astype(jnp.bfloat16), "head", scatter_dimension=1, tiled=True

time: 837 us -> 697 us (0.83)
  waiting for transfers between devices: 746 us -> 560 us
  blocking collectives: 0 us -> 40.7 us
    all_gather x1 -> x0, waiting for transfers between devices: 259 us -> none  [shards(): lax.all_gather(w_out, 'seq', axis=1, tiled=True)]
    all_to_all x1, waiting for transfers between devices: 55.5 us -> 98.9 us  [shards(): lax.all_to_all(jnp.stack([w_out] * lax.axis_size('seq')), 'seq', 0, 0)]
    all_to_all x0 -> x1, blocking collectives: none -> 40.7 us  [shards(): lax.all_to_all(for_sending(block_out), 'seq', split_axis=1, concat_axis=1...]
    unnamed x4 -> x3, waiting for transfers between devices: 98.2 us -> 127 us
  transfers between devices with their start and end apart: 6 -> 5, of which waited for: 6 -> 5; matrix products, arithmetic and copies ran while one was open for 4% -> 2% of each run, Pallas kernels for 0% -> 0%
where the time goes in v1:
time: 697 us; the launch traced here: 695 us
  waiting for transfers between devices  560 us (80%)
  blocking collectives  40.7 us (6%)
  local copies, waits for them, and re-layouts  22 us (3%)
  matrix products  21.9 us (3%)
  starting transfers between devices  18.3 us (3%)
  other arithmetic  15.6 us (2%)
  between operations  13.6 us (2%)
    all_gather x1, waiting for transfers between devices, shards(): gathered = lax.all_gather(own_queries, 'seq', axis=0, tiled=True)  319 us
    unnamed x3, waiting for transfers between devices  127 us
    all_to_all x1, waiting for transfers between devices, shards(): lax.all_to_all(jnp.stack([w_out] * lax.axis_size('seq')), 'seq', 0, 0)  98.9 us
    all_to_all x1, blocking collectives, shards(): lax.all_to_all(for_sending(block_out), 'seq', split_axis=1, concat_axis=1...  40.7 us
  transfers between devices with their start and end apart: 5, of which 5 were waited for; matrix products, arithmetic and copies ran while one was open for 2% of the time, Pallas kernels for 0%

profile of v1, /device:TPU:1, one launch (start us, length us, event | category | flops | bytes accessed | tf_op | source)
XLA Modules:
  0.0 695.5 jit_solution(2094449420156169448)
XLA Ops:
  6.5 1.8 copy.57
  8.3 0.7 fusion.24
  9.0 1.4 fusion.25
  10.4 0.3 reduce-window.12
  11.0 2.3 scatter_custom_fusion
  13.5 1.3 fusion.23
  14.8 2.3 gather_fusion
  17.1 319.4 %all-gather.3.cloned.1.call-done = bf16[2048,640]{1,0:T(8,128)(2,1)} async-done(((bf16[32,640]{1,0:T(8,128)(2,1)}), bf16[2048,640]{1,0:T(8,128)(2,1)}) %all-gather.3.cloned.1.call-update) | async-done | bytes 2621456 | tf_op jit(solution)/shard_map/all_gather | solution.py:49
  336.6 25.7 %while.14 = (s32[]{:T(128)}, bf16[5,2048,128]{2,1,0:T(8,128)(2,1)S(1)}, f32[5,2048]{1,0:T(8,128)S(1)}, f32[5,2048]{1,0:T(8,128)S(1)}, s32[5]{0:T(128)S(1)}, /*in...) while((s32[]{:T(128)}, ...), condition=%wide.region_8.9_spmd, body=%wide.region_5.8_spmd.sunk | while | flops 272101376 | bytes 7546555 | solution.py:38
  336.6 0.6 dynamic_slice.30
  337.8 1.5 fusion.39
  339.3 0.3 fusion.40
  339.6 1.6 fusion.41
  341.3 0.2 dynamic_update_slice.17
  341.5 0.2 dynamic_update_slice.16
  341.7 0.6 dynamic_slice.30
  342.9 1.5 fusion.39
  344.4 0.3 fusion.40
  344.8 1.6 fusion.41
  346.4 0.2 dynamic_update_slice.17
  346.6 0.2 dynamic_update_slice.16
  346.8 0.6 dynamic_slice.30
  348.1 1.5 fusion.39
  349.6 0.3 fusion.40
  349.9 1.6 fusion.41
  351.5 0.2 dynamic_update_slice.17
  351.7 0.2 dynamic_update_slice.16
  352.0 0.6 dynamic_slice.30
  353.2 1.5 fusion.39
  354.7 0.3 fusion.40
  355.0 1.6 fusion.41
  356.7 0.2 dynamic_update_slice.17
  356.9 0.2 dynamic_update_slice.16
  357.1 0.6 dynamic_slice.30
  358.4 1.5 fusion.39
  359.9 0.3 fusion.40
  360.2 1.6 fusion.41
  361.8 0.2 dynamic_update_slice.17
  362.5 1.1 reshape.206
  363.5 7.6 %all-to-all-start.2 = ((f32[64,1,160]{2,1,0:T(1,128)}), f32[64,1,160]{2,1,0:T(1,128)S(1)}, u32[]{:S(2)}, u32[]{:S(2)}) async-start(f32[64,1,160]{2,1,0:T(1,128)} %reshape.206), calls=%async_computation.2 | async-start | bytes 131072 | tf_op jit(solution)/shard_map/all_to_all | solution.py:53
  371.4 0.8 reshape.204
  372.1 7.9 %all-to-all-done.2 = f32[64,1,160]{2,1,0:T(1,128)S(1)} async-done(((f32[64,1,160]{2,1,0:T(1,128)}), f32[64,1,160]{2,1,0:T(1,128)S(1)}, u32[]{:S(2)}, u32[]{:S(2)}) %all-to-all-start.2) | async-done | bytes 40992 | tf_op jit(solution)/shard_map/all_to_all | solution.py:53
  380.0 4.6 all-to-all-start.1
  384.7 2.2 copy.17
  386.9 6.6 all-to-all-done.1
  393.5 40.7 %all_to_all.20 = bf16[5,64,32,128]{3,2,0,1:T(8,128)(2,1)} all-to-all(bf16[5,64,32,128]{3,2,0,1:T(8,128)(2,1)S(1)} %copy.17), channel_id=1, replica_groups=mesh['seq'=64,'head'=8] {'seq'}, dimensions={1} | all-to-all | bytes 5242880 | tf_op jit(solution)/shard_map/all_to_all | solution.py:68
  434.2 3.2 stack.2
  437.4 5.8 all-to-all-start.3
  443.2 0.2 reduce-scatter.4.cloned.1.call-start
  443.5 0.5 broadcast.204
  444.0 0.8 reduce.6
  444.9 0.8 reduce.7
  445.8 0.7 bitcast_reduce_fusion
  446.4 1.4 fusion.16
  447.8 1.1 copy.23
  448.9 1.3 fusion.15
  450.2 0.8 copy.21
  451.0 1.4 fusion.12
  452.6 98.9 %all-to-all-done.3 = bf16[64,640,80]{1,2,0:T(8,128)(2,1)} async-done(((bf16[64,640,80]{1,2,0:T(8,128)(2,1)}), bf16[64,640,80]{1,2,0:T(8,128)(2,1)}, u32[]{:S(2)}, u32[]{:S(2)}) %all-to-all-start.3) | async-done | bytes 6553632 | tf_op jit(solution)/shard_map/all_to_all | solution.py:79
  551.5 4.9 convolution_convert_fusion
  556.4 1.4 copy.25
  557.9 127.0 %reduce-scatter.4.cloned.1.call-done = bf16[640,32]{1,0:T(8,128)(2,1)} async-done(((bf16[5120,32]{1,0:T(8,128)(2,1)}), bf16[640,32]{1,0:T(8,128)(2,1)}) %reduce-scatter.4.cloned.1.call-update) | async-done | bytes 40976
  684.9 1.0 copy.26
  685.9 2.7 scatter_custom_fusion.1
  (36 shorter events, 1.5 us)
Async XLA Ops:
  6.5 679.4 %copy-start = (bf16[256,640]{1,0:T(8,128)(2,1)S(1)}, bf16[256,640]{1,0:T(8,128)(2,1)}, u32[]{:S(2)}) copy-start(bf16[256,640]{1,0:T(8,128)(2,1)} %param.12) | copy-start | bytes 983044
  6.5 330.0 %all-gather.3.cloned.1.call-start = ((), (), s32[]{:S(2)}) async-start(), calls=%async_computation.5 | async-start | bytes 2662400 | tf_op jit(solution)/shard_map/all_gather | solution.py:49
  14.8 2.3 copy-start.4
  362.2 22.4 %copy-start.2 = (bf16[5,2048,128]{2,1,0:T(8,128)(2,1)}, bf16[5,2048,128]{2,1,0:T(8,128)(2,1)S(1)}, u32[]{:S(2)}) copy-start(bf16[5,2048,128]{2,1,0:T(8,128)(2,1)S(1)} %get-tuple-element.49) | copy-start | bytes 7864324
  363.5 16.5 %all-to-all-start.2 = ((f32[64,1,160]{2,1,0:T(1,128)}), f32[64,1,160]{2,1,0:T(1,128)S(1)}, u32[]{:S(2)}, u32[]{:S(2)}) async-start(f32[64,1,160]{2,1,0:T(1,128)} %reshape.206), calls=%async_computation.2 | async-start | bytes 131072 | tf_op jit(solution)/shard_map/all_to_all | solution.py:53
  380.0 13.5 %all-to-all-start.1 = ((f32[64,1,160]{2,1,0:T(1,128)}), f32[64,1,160]{2,1,0:T(1,128)S(1)}, u32[]{:S(2)}, u32[]{:S(2)}) async-start(f32[64,1,160]{2,1,0:T(1,128)} %reshape.204), calls=%async_computation.1 | async-start | bytes 131072 | tf_op jit(solution)/shard_map/all_to_all | solution.py:60
  386.8 47.3 %copy-start.3 = (bf16[640,80]{0,1:T(8,128)(2,1)S(1)}, bf16[640,80]{0,1:T(8,128)(2,1)}, u32[]{:S(2)}) copy-start(bf16[640,80]{0,1:T(8,128)(2,1)} %param.15) | copy-start | bytes 307204
  437.4 13.6 %copy-start.1 = (bf16[5,64,32,128]{3,2,0,1:T(8,128)(2,1)S(1)}, bf16[5,64,32,128]{3,2,0,1:T(8,128)(2,1)}, u32[]{:S(2)}) copy-start(bf16[5,64,32,128]{3,2,0,1:T(8,128)(2,1)} %all_to_all.20) | copy-start | bytes 7864324
  437.4 114.1 %all-to-all-start.3 = ((bf16[64,640,80]{1,2,0:T(8,128)(2,1)}), bf16[64,640,80]{1,2,0:T(8,128)(2,1)}, u32[]{:S(2)}, u32[]{:S(2)}) async-start(bf16[64,640,80]{1,2,0:T(8,128)(2,1)} %stack.2), calls=%async_computation.3 | async-start | bytes 13107200 | tf_op jit(solution)/shard_map/all_to_all | solution.py:79
  443.2 241.6 %reduce-scatter.4.cloned.1.call-start = ((), (), s32[]{:S(2)}) async-start(), calls=%async_computation.6 | async-start | bytes 1474560
  556.4 129.5 %copy-start.5 = (s32[1024]{0:T(1024)S(1)}, s32[1024]{0:T(1024)}, u32[]{:S(2)}) copy-start(s32[1024]{0:T(1024)} %copy-done.4) | copy-start | bytes 12292
Sparse Core Ops, SparseCore 0:
  17.2 319.2 all-gather.2
  558.0 126.8 reduce-scatter.3
